TPU v7x, 256 devices: a whole 4x4x8 slice. The times are simulated.
256 devices in a mesh: layer: 4 (over z_lo, core), latent: 64 (over x, y, z_hi).
Axes of the slice: x: 4, y: 4, z: 8 (z_hi: 4, z_lo: 2; z = z_hi * 2 + z_lo), core: 2. Of those that a mesh axis runs over, the one named last changes fastest.
Arguments:
- streams: bfloat16 [4, 1024, 4096], P('layer', 'latent'), may hold values from -6 to 6
- enc_weight: bfloat16 [4, 4096, 32768], P('layer', None, 'latent'), may hold values from -0.046875 to 0.046875
- enc_bias: float32 [32768], P('latent'), may hold values from -3 to 3
- dec_weight: bfloat16 [4, 32768, 4096], P('layer', 'latent'), may hold values from -0.046875 to 0.046875
- dec_bias: float32 [4, 4096], P('layer'), may hold values from -3 to 3
Outputs:
- recon: float32 [4, 1024, 4096], P('layer', 'latent')
All inputs are finite; a program needn't handle non-finite values.
Results may differ from a plain program's by a relative error of at most 0.0027.
Values may be sent and summed in bfloat16 or wider, within the bound.
A program may use at most 128 MiB of HBM per device.

v0:
```python
import jax
import jax.numpy as jnp
from jax import lax
from jax.sharding import PartitionSpec as P


def shards(streams, enc_weight, enc_bias, dec_weight, dec_bias):
    partial_value = jnp.einsum(
        "ltd,ldm->tm",
        lax.all_gather(streams, "latent", axis=1, tiled=True),
        enc_weight,
        preferred_element_type=jnp.float32,
    )
    summed = lax.psum(partial_value, "layer")
    codes = jnp.maximum(summed + enc_bias[None, :], 0.0).astype(jnp.bfloat16)
    summed_rows = lax.psum_scatter(
        jnp.einsum("tm,lmd->tld", codes, dec_weight, preferred_element_type=jnp.float32),
        "latent",
        scatter_dimension=0,
        tiled=True,
    )
    return jnp.transpose(summed_rows, (1, 0, 2)) + dec_bias[:, None, :]


def solution(mesh):
    in_specs = (
        P("layer", "latent", None),
        P("layer", None, "latent"),
        P("latent"),
        P("layer", "latent", None),
        P("layer", None),
    )
    out_specs = P("layer", "latent", None)
    return jax.shard_map(shards, mesh=mesh, in_specs=in_specs, out_specs=out_specs, check_vma=False)
```

profile of v0, /device:TPU:64, one launch (start us, length us, event | category | flops | bytes accessed | tf_op | source)
XLA Modules:
  0.0 705.1 jit_solution(15670505570058612425)
XLA Ops:
  6.5 0.0 all-gather.2.cloned.1.call-start
  6.5 0.7 all-gather.2.cloned.1.call-update
  7.3 0.0 copy-start.1
  7.3 0.0 all-reduce.2.cloned.1.call-start
  7.3 120.3 %all-gather.2.cloned.1.call-done = bf16[1,1024,4096]{2,1,0:T(8,128)(2,1)} async-done(((bf16[1,16,4096]{2,1,0:T(8,128)(2,1)}), bf16[1,1024,4096]{2,1,0:T(8,128)(2,1)}) %all-gather.2.cloned.1.call-update) | async-done | bytes 8388624 | tf_op jit(solution)/shard_map/all_gather | solution.py:10
  127.6 10.4 %fusion = f32[1024,512]{1,0:T(8,128)} fusion(bf16[1,1024,4096]{2,1,0:T(8,128)(2,1)} %all-gather.2.cloned.1.call-done, bf16[1,4096,512]{2,1,0:T(8,128)(2,1)} %param.6), kind=kOutput, calls=%fused_computation.1 | convolution fusion | flops 4294967296 | bytes 14680064 | tf_op jit(solution)/shard_map/ltd,ldm->tm/dot_general | solution.py:8
  138.1 0.0 all-reduce.2.cloned.1.call-update
  138.1 0.0 reduce-scatter.2.cloned.1.call-start
  138.1 60.6 %all-reduce.2.cloned.1.call-done = f32[1024,512]{1,0:T(8,128)} async-done(((f32[1024,512]{1,0:T(8,128)}), f32[1024,512]{1,0:T(8,128)}) %all-reduce.2.cloned.1.call-update) | async-done | bytes 2097168 | tf_op jit(solution)/shard_map/psum | solution.py:14
  198.7 0.0 copy-done.1
  198.7 13.1 %convolution_bitcast_fusion = f32[1024,1,4096]{2,0,1:T(8,128)} fusion(bf16[1,512,4096]{2,1,0:T(8,128)(2,1)} %param.8, f32[1024,512]{1,0:T(8,128)} %all-reduce.2.cloned.1.call-done, f32[512]{0:T(512)S(1)} %copy-done.1), kind=kOutput, calls=%fused_computation | convolution fusion | flops 4296540160 | bytes 23070720 | tf_op jit(solution)/shard_map/tm,lmd->tld/dot_general | solution.py:17
  211.8 0.0 copy-start
  211.8 0.0 reduce-scatter.2.cloned.1.call-update
  211.8 485.0 %reduce-scatter.2.cloned.1.call-done = f32[16,1,4096]{2,0,1:T(8,128)} async-done(((f32[1024,1,4096]{2,0,1:T(8,128)}), f32[16,1,4096]{2,0,1:T(8,128)}) %reduce-scatter.2.cloned.1.call-update) | async-done | bytes 262160 | tf_op jit(solution)/shard_map/reduce_scatter | solution.py:16
  696.9 0.0 copy-done
  696.9 1.7 bitcast_add_fusion
Async XLA Ops:
  6.5 121.1 %all-gather.2.cloned.1.call-start = ((), (), s32[]{:S(2)}) async-start(), calls=%async_computation.1 | async-start | bytes 8519680 | tf_op jit(solution)/shard_map/all_gather | solution.py:10
  7.3 191.5 %copy-start.1 = (f32[512]{0:T(512)S(1)}, f32[512]{0:T(512)}, u32[]{:S(2)}) copy-start(f32[512]{0:T(512)} %param.7) | copy-start | bytes 6148
  7.3 191.5 %all-reduce.2.cloned.1.call-start = ((), (), s32[]{:S(2)}) async-start(), calls=%async_computation.2 | async-start | bytes 4194304 | tf_op jit(solution)/shard_map/psum | solution.py:14
  138.1 558.8 %reduce-scatter.2.cloned.1.call-start = ((), (), s32[]{:S(2)}) async-start(), calls=%async_computation.3 | async-start | bytes 17039360 | tf_op jit(solution)/shard_map/reduce_scatter | solution.py:16
  211.8 485.1 %copy-start = (f32[1,4096]{1,0:T(1,128)S(1)}, f32[1,4096]{1,0:T(1,128)}, u32[]{:S(2)}) copy-start(f32[1,4096]{1,0:T(1,128)} %param.9) | copy-start | bytes 49156
Sparse Core Ops, SparseCore 0:
  10.7 116.9 all-gather.1
  138.2 60.4 all-reduce.1
  211.9 484.8 reduce-scatter.1
where the time goes:
time: 705 us
  waiting for transfers between devices  667 us (95%)
  matrix products  23.5 us (3%)
  between operations  13.1 us (2%)
    reduce_scatter x1, waiting for transfers between devices, shards(): lax.psum_scatter(jnp.einsum('tm,lmd->tld', codes, dec_weight, preferred_e...  485 us
    all_gather x1, waiting for transfers between devices, shards(): lax.all_gather(streams, 'latent', axis=1, tiled=True)  120 us
    psum x1, waiting for transfers between devices, shards(): summed = lax.psum(partial_value, 'layer')  60.6 us
  transfers between devices with their start and end apart: 3, of which 3 were waited for; matrix products, arithmetic and copies ran while one was open for 0% of the time, Pallas kernels for 0%

commit v1 on v0

v1 whole, which is shorter than its diff:
```python
import functools

import jax
import jax.numpy as jnp
from jax import lax
from jax.experimental import pallas as pl
from jax.experimental.pallas import tpu as pltpu
from jax.sharding import PartitionSpec as P

MESH = pl.DeviceIdType.MESH
F32, BF16 = jnp.float32, jnp.bfloat16
OFF = (0, 1, 3, 2)
NK = 4
ROWS, D, M, HALF = 16, 4096, 512, 2048
A_STEPS = (1, 3, 2)

PROGRAM = (
    "A0", "Z", "B02", "B00", "C00", "B01", "C01", "C02", "A1", "C03", "A2", "A3",
    "B10", "B12", "B11", "D0", "B21", "B20", "B22", "C13", "C10", "X0", "C11", "C12",
    "C23", "C22", "C21", "C20", "B30", "B32", "Y0", "D1", "X1", "B31", "E00", "E01",
    "D2", "X2", "C31", "C33", "C32", "C30", "Y1", "E10", "E11", "D3", "F011", "F010",
    "Y2", "F000", "F001", "F100", "F111", "F101", "F110", "X3", "G01", "G00", "G11", "G10",
    "H00", "E20", "H01", "E21", "Y3", "H11", "H10", "E30", "E31", "F200", "F201", "F210",
    "F211", "F301", "F300", "G20", "G21", "F310", "F311", "H20", "G30", "H21", "G31", "H30",
    "H31",
)


def kernel(
    s_ref, we_hbm, eb_ref, wd_hbm, out_ref,
    g, we, wd, part, cx, q, zx, codes, full, ob, r1, r2, asnd, arcv, zsnd, zrcv, acc,
    lsem, ag_s, ag_r, zg_s, zg_r, x_s, x_r, rs_s, rs_r,
):
    lay, lat = lax.axis_index("layer"), lax.axis_index("latent")
    zlo, core = lay // 2, lay % 2
    x, y, z = lat // 16, (lat // 4) % 4, lat % 4
    m4 = lambda v: lax.rem(v + 8, 4)

    def dev(dx=0, dy=0, dz=0, dl=0, dc=0):
        return (
            lax.rem(zlo + dl, 2) * 2 + lax.rem(core + dc, 2),
            (m4(x + dx) * 4 + m4(y + dy)) * 4 + m4(z + dz),
        )

    def a_dev(h, d):
        return dev(dy=d) if h == 0 else dev(dx=d)

    def b_dev(h, d):
        return dev(dx=d) if h == 0 else dev(dy=d)

    ca = (y, x)
    cb = (x, y)
    cols = tuple(pl.ds(h * HALF, HALF) for h in range(2))

    def slot(buf, k, h, b, a):
        return buf.at[k, b, a, :, cols[h]] if h == 0 else buf.at[k, a, b, :, cols[h]]

    def span(buf, k, h, b, a0, n):
        return buf.at[k, b, pl.ds(a0, n), :, cols[h]] if h == 0 else buf.at[k, pl.ds(a0, n), b, :, cols[h]]

    def push(src, dst, ssem, rsem, target):
        return pltpu.make_async_remote_copy(
            src_ref=src, dst_ref=dst, send_sem=ssem, recv_sem=rsem, device_id=target, device_id_type=MESH
        )

    sent = []

    def start(copy):
        copy.start()
        sent.append(copy)

    load_s = pltpu.make_async_copy(s_ref.at[0], g.at[0, x, y], lsem.at[0])
    load_e = pltpu.make_async_copy(we_hbm.at[0], we, lsem.at[1])
    load_d = pltpu.make_async_copy(wd_hbm.at[0], wd, lsem.at[2])
    load_s.start()
    load_e.start()
    load_d.start()
    bar = pltpu.get_barrier_semaphore()
    partners = [dev(dx=d) for d in (1, 2, 3)] + [dev(dy=d) for d in (1, 2, 3)]
    partners += [dev(dz=d) for d in (1, 2, 3)] + [dev(dc=1), dev(dl=1)]
    for p in partners:
        pl.semaphore_signal(bar, inc=1, device_id=p, device_id_type=MESH)
    pl.semaphore_wait(bar, len(partners))
    load_s.wait()

    def zg(k):
        return push(g.at[0, x, y], g.at[k, x, y], zg_s.at[k], zg_r.at[k], dev(dz=4 - OFF[k]))

    def ag(k, h, i):
        a, b = ca[h], cb[h]
        if i < 3:
            src, target = slot(g, k, h, b, a), a_dev(h, A_STEPS[i])
        elif i < 11:
            j, way = (i - 3) // 2, (i - 3) % 2
            src, target = slot(g, k, h, b, m4(a + j)), b_dev(h, 1 if way == 0 else 3)
        else:
            j = i - 11
            src = slot(g, k, h, m4(b + (3 if j % 2 == 0 else 1)), m4(a + j))
            target = b_dev(h, 1 if j % 2 == 0 else 3)
        return push(src, src, ag_s.at[k, h, i], ag_r.at[k, h, i], target)

    def step_z():
        for i in range(1, NK):
            start(zg(i))

    def step_a(k):
        if k:
            zg(k).wait_recv()
        for h in range(2):
            for i in (0, 1, 3, 4, 2):
                start(ag(k, h, i))

    def step_b(k, i):
        j = (4 - A_STEPS[i]) % 4
        for h in range(2):
            ag(k, h, i).wait_recv()
            start(ag(k, h, 3 + 2 * j))
            start(ag(k, h, 4 + 2 * j))

    def step_c(k, j):
        for h in range(2):
            ag(k, h, 3 + 2 * j + j % 2).wait_recv()
            start(ag(k, h, 11 + j))

    def step_w(k):
        for h in range(2):
            for j in range(4):
                ag(k, h, 3 + 2 * j + 1 - j % 2).wait_recv()
        for h in range(2):
            for j in range(4):
                ag(k, h, 11 + j).wait_recv()

    def xch(k, i):
        if i == 0:
            return push(part.at[k, 1 - core], cx.at[k], x_s.at[k, 0], x_r.at[k, 0], dev(dc=1))
        if i == 1:
            return push(q.at[k], zx.at[k], x_s.at[k, 1], x_r.at[k, 1], dev(dl=1))
        mine = codes.at[k, pl.ds(2 * core, 2)]
        return push(mine, mine, x_s.at[k, 2], x_r.at[k, 2], dev(dc=1))

    loaded = []

    def step_d(k):
        step_w(k)
        if not loaded:
            load_e.wait()
            load_d.wait()
            loaded.append(k)
        rows = g.at[k]

        def body(n, c):
            at = pl.ds(pl.multiple_of(n * 256, 256), 256)
            lhs = rows[...].reshape(256, D)
            r = jnp.dot(lhs, we[:, at], preferred_element_type=F32)
            part[k, :, :, at] = r.reshape(2, 128, 256)
            return c

        lax.fori_loop(0, 2, body, 0)
        start(xch(k, 0))

    def step_x(k):
        xch(k, 0).wait_recv()
        q[k] = part[k, core] + cx[k]
        start(xch(k, 1))

    def step_y(k):
        xch(k, 1).wait_recv()
        pre = q[k] + zx[k] + eb_ref[...]
        codes[k, pl.ds(2 * core, 2)] = jnp.maximum(pre, 0.0).astype(BF16).reshape(2, 4, ROWS, M)
        start(xch(k, 2))

    def rs(k, h, i):
        a, b = ca[h], cb[h]
        if i == 0:
            src, dst, t = span(ob, k, h, m4(b + 2), 0, 2), r1.at[k, h, 0], b_dev(h, 1)
        elif i == 1:
            src, dst, t = span(ob, k, h, m4(b + 2), 2, 2), r1.at[k, h, 1], b_dev(h, 3)
        elif i == 2:
            src, dst, t = span(ob, k, h, m4(b + 1), 2, 2), r2.at[k, h, 0, pl.ds(2, 2)], b_dev(h, 1)
        elif i == 3:
            src, dst, t = span(ob, k, h, m4(b + 3), 0, 2), r2.at[k, h, 1, pl.ds(0, 2)], b_dev(h, 3)
        elif i == 4:
            src, dst, t = span(ob, k, h, m4(b + 1), 0, 2), r2.at[k, h, 0, pl.ds(0, 2)], b_dev(h, 1)
        elif i == 5:
            src, dst, t = span(ob, k, h, m4(b + 3), 2, 2), r2.at[k, h, 1, pl.ds(2, 2)], b_dev(h, 3)
        elif i < 9:
            d = A_STEPS[i - 6]
            src, dst, t = asnd.at[k, h, m4(a + d)], arcv.at[k, h, i - 6], a_dev(h, d)
        else:
            src, dst, t = zsnd.at[k, :, cols[h]], zrcv.at[k, :, cols[h]], dev(dz=OFF[k])
        return push(src, dst, rs_s.at[k, h, i], rs_r.at[k, h, i], t)

    def step_e(k, h):
        if h == 0:
            xch(k, 2).wait_recv()

        def body(n, c):
            at = pl.ds(pl.multiple_of(h * HALF + n * 512, 512), 512)
            r = jnp.dot(codes[k].reshape(256, M), wd[:, at], preferred_element_type=F32)
            r = r.reshape(4, 4, ROWS, 512)
            full[k % 2, :, :, :, at] = r
            ob[k, :, :, :, at] = r.astype(BF16)
            return c

        lax.fori_loop(0, HALF // 512, body, 0)
        for i in range(4):
            start(rs(k, h, i))

    def tiles(width, step, body):
        def run(n, c):
            body(pl.multiple_of(n * step, step))
            return c

        lax.fori_loop(0, width // step, run, 0)

    def step_f(k, h, w):
        rs(k, h, w).wait_recv()
        to = m4(cb[h] + (1 if w == 0 else 3))
        rows = pl.ds(0 if w == 0 else 2, 2)

        def body(c0):
            at = pl.ds(h * HALF + c0, 512)
            got = r1[k, h, w, :, :, pl.ds(c0, 512)].astype(F32)
            if h == 0:
                ob[k, to, rows, :, at] = (full[k % 2, to, rows, :, at] + got).astype(BF16)
            else:
                ob[k, rows, to, :, at] = (full[k % 2, rows, to, :, at] + got).astype(BF16)

        tiles(HALF, 512, body)
        start(rs(k, h, 4 + w))

    def step_g(k, h):
        for i in (2, 3, 4, 5):
            rs(k, h, i).wait_recv()
        b = cb[h]

        def body(c0):
            at = pl.ds(h * HALF + c0, 512)
            got = r2[k, h, 0, :, :, pl.ds(c0, 512)].astype(F32) + r2[k, h, 1, :, :, pl.ds(c0, 512)].astype(F32)
            if h == 0:
                s = full[k % 2, b, :, :, at] + got
                full[k % 2, b, :, :, at] = s
            else:
                s = full[k % 2, :, b, :, at] + got
                full[k % 2, :, b, :, at] = s
            asnd[k, h, :, :, pl.ds(c0, 512)] = s.astype(BF16)

        tiles(HALF, 512, body)
        for i in (6, 7, 8):
            start(rs(k, h, i))

    def step_h(k, h):
        for i in (6, 7, 8):
            rs(k, h, i).wait_recv()
        at = cols[h]
        s = full[k % 2, x, y, :, at]
        for i in range(3):
            s = s + arcv[k, h, i].astype(F32)
        if k == 0:
            acc[:, at] = s
        else:
            zsnd[k, :, at] = s.astype(BF16)
            start(rs(k, h, 9))

    steps = dict(
        Z=step_z, A=step_a, B=step_b, C=step_c, D=step_d, X=step_x, Y=step_y, E=step_e, F=step_f, G=step_g, H=step_h
    )
    for name in PROGRAM:
        steps[name[0]](*(int(v) for v in name[1:]))

    for k in range(1, NK):
        for h in range(2):
            rs(k, h, 9).wait_recv()
    total = acc[...]
    for k in range(1, NK):
        total = total + zrcv[k].astype(F32)
    out_ref[...] = total
    for copy in sent:
        copy.wait_send()


def shards(streams, enc_weight, enc_bias, dec_weight, dec_bias):
    dma = pltpu.SemaphoreType.DMA
    any_space, vmem = pl.BlockSpec(memory_space=pl.ANY), pl.BlockSpec(memory_space=pltpu.VMEM)
    rows = pl.pallas_call(
        kernel,
        out_shape=jax.ShapeDtypeStruct((ROWS, D), F32),
        in_specs=[any_space, any_space, vmem, any_space],
        out_specs=vmem,
        scratch_shapes=[
            pltpu.VMEM((NK, 4, 4, ROWS, D), BF16),
            pltpu.VMEM((D, M), BF16),
            pltpu.VMEM((M, D), BF16),
            pltpu.VMEM((NK, 2, 128, M), F32),
            pltpu.VMEM((NK, 128, M), F32),
            pltpu.VMEM((NK, 128, M), F32),
            pltpu.VMEM((NK, 128, M), F32),
            pltpu.VMEM((NK, 4, 4, ROWS, M), BF16),
            pltpu.VMEM((2, 4, 4, ROWS, D), F32),
            pltpu.VMEM((NK, 4, 4, ROWS, D), BF16),
            pltpu.VMEM((NK, 2, 2, 2, ROWS, HALF), BF16),
            pltpu.VMEM((NK, 2, 2, 4, ROWS, HALF), BF16),
            pltpu.VMEM((NK, 2, 4, ROWS, HALF), BF16),
            pltpu.VMEM((NK, 2, 3, ROWS, HALF), BF16),
            pltpu.VMEM((NK, ROWS, D), BF16),
            pltpu.VMEM((NK, ROWS, D), BF16),
            pltpu.VMEM((ROWS, D), F32),
            dma((3,)),
            dma((NK, 2, 15)),
            dma((NK, 2, 15)),
            dma((NK,)),
            dma((NK,)),
            dma((NK, 3)),
            dma((NK, 3)),
            dma((NK, 2, 10)),
            dma((NK, 2, 10)),
        ],
        compiler_params=pltpu.CompilerParams(
            collective_id=1, has_side_effects=True, vmem_limit_bytes=60 * 1024 * 1024
        ),
        cost_estimate=pl.CostEstimate(flops=8 * 1024 * D * M, bytes_accessed=9 * 1024 * 1024, transcendentals=0),
        name="crosscoder",
    )(streams, enc_weight, enc_bias.reshape(1, M), dec_weight)
    return (rows + dec_bias)[None]


def solution(mesh):
    in_specs = (
        P("layer", "latent", None),
        P("layer", None, "latent"),
        P("latent"),
        P("layer", "latent", None),
        P("layer", None),
    )
    return jax.shard_map(
        shards, mesh=mesh, in_specs=in_specs, out_specs=P("layer", "latent", None), check_vma=False
    )
```

time: 705 us -> 125 us (0.18)
  the two profiles are of different devices: /device:TPU:64 before, /device:TPU:1 now
where the time goes in v1:
time: 125 us; the launch traced here: 122 us
  Pallas kernels  121 us (97%)
  other arithmetic  1.68 us (1%)
    pallas_call x1, Pallas kernels, shards(): pl.pallas_call(kernel, out_shape=jax.ShapeDtypeStruct((ROWS, D), F32), in...  121 us

profile of v1, /device:TPU:1, one launch (start us, length us, event | category | flops | bytes accessed | tf_op | source)
XLA Modules:
  0.0 122.3 jit_solution(981852673536929232)
XLA Ops:
  0.0 0.0 copy-start
  0.0 120.6 %crosscoder.1 = f32[16,4096]{1,0:T(8,128)} custom-call(bf16[1,16,4096]{2,1,0:T(8,128)(2,1)} %s_ref.1, bf16[1,4096,512]{2,1,0:T(8,128)(2,1)} %we_hbm.1, f32[1,512]{1,0:T(1,128)} %bitcast.5, bf16[1,512,4096]{2,1,0:T(8,128)(2,1)} %wd_hbm.1), custom_call_target="tpu_custom_call" | custom-call | flops 17179869184 | bytes 9437184 | tf_op jit(solution)/shard_map/crosscoder/pallas_call | solution.py:285
  120.6 0.0 copy-done
  120.6 1.7 %add_bitcast_fusion = f32[1,16,4096]{2,1,0:T(8,128)} fusion(f32[16,4096]{1,0:T(8,128)} %crosscoder.1, f32[4096]{0:T(1024)S(1)} %bitcast.4), kind=kLoop, calls=%fused_computation | loop fusion | flops 65536 | bytes 540672 | tf_op jit(solution)/shard_map/broadcast_in_dim | solution.py:324
Async XLA Ops:
  0.0 120.6 %copy-start = (f32[1,4096]{1,0:T(1,128)S(1)}, f32[1,4096]{1,0:T(1,128)}, u32[]{:S(2)}) copy-start(f32[1,4096]{1,0:T(1,128)} %param.9) | copy-start | bytes 49156

commit v2 on v1

--- a/solution.py
+++ b/solution.py
@@ -15,14 +15,14 @@
 A_STEPS = (1, 3, 2)
 
 PROGRAM = (
-    "A0", "Z", "B02", "B00", "C00", "B01", "C01", "C02", "A1", "C03", "A2", "A3",
-    "B10", "B12", "B11", "D0", "B21", "B20", "B22", "C13", "C10", "X0", "C11", "C12",
-    "C23", "C22", "C21", "C20", "B30", "B32", "Y0", "D1", "X1", "B31", "E00", "E01",
-    "D2", "X2", "C31", "C33", "C32", "C30", "Y1", "E10", "E11", "D3", "F011", "F010",
-    "Y2", "F000", "F001", "F100", "F111", "F101", "F110", "X3", "G01", "G00", "G11", "G10",
-    "H00", "E20", "H01", "E21", "Y3", "H11", "H10", "E30", "E31", "F200", "F201", "F210",
-    "F211", "F301", "F300", "G20", "G21", "F310", "F311", "H20", "G30", "H21", "G31", "H30",
-    "H31",
+    "Z2", "A0", "Z1", "B00", "B01", "A1", "B02", "A2", "C00", "B10", "Z3", "B11",
+    "C03", "C01", "C02", "B12", "A3", "B20", "C11", "C13", "C12", "C10", "D0", "X0",
+    "B31", "B30", "B21", "B32", "D1", "C33", "C31", "B22", "Y0", "X1", "C30", "C32",
+    "C21", "C22", "C20", "C23", "E00", "E01", "D3", "Y1", "X3", "E10", "E11", "D2",
+    "X2", "F010", "F000", "F011", "Y3", "F001", "E30", "E31", "Y2", "E20", "E21", "F101",
+    "F100", "F300", "F310", "F301", "F311", "F111", "F110", "F201", "F200", "F211", "F210", "G31",
+    "G30", "G20", "G11", "H31", "G10", "H30", "G21", "H20", "H11", "H21", "H10", "G01",
+    "G00", "H01", "H00",
 )
 
 
@@ -88,8 +88,13 @@
 
     def ag(k, h, i):
         a, b = ca[h], cb[h]
-        if i < 3:
+        if i < 2:
             src, target = slot(g, k, h, b, a), a_dev(h, A_STEPS[i])
+        elif i == 2 or i == 15:
+            from_a, w = (m4(a + 3), 0) if i == 2 else (m4(a + 1), 1)
+            at = pl.ds(h * HALF + w * (HALF // 2), HALF // 2)
+            src = g.at[k, b, from_a, :, at] if h == 0 else g.at[k, from_a, b, :, at]
+            target = a_dev(h, 1 if i == 2 else 3)
         elif i < 11:
             j, way = (i - 3) // 2, (i - 3) % 2
             src, target = slot(g, k, h, b, m4(a + j)), b_dev(h, 1 if way == 0 else 3)
@@ -99,21 +104,24 @@
             target = b_dev(h, 1 if j % 2 == 0 else 3)
         return push(src, src, ag_s.at[k, h, i], ag_r.at[k, h, i], target)
 
-    def step_z():
-        for i in range(1, NK):
-            start(zg(i))
+    def step_z(k):
+        start(zg(k))
 
     def step_a(k):
         if k:
             zg(k).wait_recv()
         for h in range(2):
-            for i in (0, 1, 3, 4, 2):
+            for i in (0, 1, 3, 4):
                 start(ag(k, h, i))
 
     def step_b(k, i):
         j = (4 - A_STEPS[i]) % 4
         for h in range(2):
             ag(k, h, i).wait_recv()
+            if i == 2:
+                ag(k, h, 15).wait_recv()
+            else:
+                start(ag(k, h, 2 if i == 0 else 15))
             start(ag(k, h, 3 + 2 * j))
             start(ag(k, h, 4 + 2 * j))
 
@@ -198,7 +206,7 @@
             at = pl.ds(pl.multiple_of(h * HALF + n * 512, 512), 512)
             r = jnp.dot(codes[k].reshape(256, M), wd[:, at], preferred_element_type=F32)
             r = r.reshape(4, 4, ROWS, 512)
-            full[k % 2, :, :, :, at] = r
+            full[k, :, :, :, at] = r
             ob[k, :, :, :, at] = r.astype(BF16)
             return c
 
@@ -222,9 +230,9 @@
             at = pl.ds(h * HALF + c0, 512)
             got = r1[k, h, w, :, :, pl.ds(c0, 512)].astype(F32)
             if h == 0:
-                ob[k, to, rows, :, at] = (full[k % 2, to, rows, :, at] + got).astype(BF16)
+                ob[k, to, rows, :, at] = (full[k, to, rows, :, at] + got).astype(BF16)
             else:
-                ob[k, rows, to, :, at] = (full[k % 2, rows, to, :, at] + got).astype(BF16)
+                ob[k, rows, to, :, at] = (full[k, rows, to, :, at] + got).astype(BF16)
 
         tiles(HALF, 512, body)
         start(rs(k, h, 4 + w))
@@ -238,11 +246,11 @@
             at = pl.ds(h * HALF + c0, 512)
             got = r2[k, h, 0, :, :, pl.ds(c0, 512)].astype(F32) + r2[k, h, 1, :, :, pl.ds(c0, 512)].astype(F32)
             if h == 0:
-                s = full[k % 2, b, :, :, at] + got
-                full[k % 2, b, :, :, at] = s
+                s = full[k, b, :, :, at] + got
+                full[k, b, :, :, at] = s
             else:
-                s = full[k % 2, :, b, :, at] + got
-                full[k % 2, :, b, :, at] = s
+                s = full[k, :, b, :, at] + got
+                full[k, :, b, :, at] = s
             asnd[k, h, :, :, pl.ds(c0, 512)] = s.astype(BF16)
 
         tiles(HALF, 512, body)
@@ -253,7 +261,7 @@
         for i in (6, 7, 8):
             rs(k, h, i).wait_recv()
         at = cols[h]
-        s = full[k % 2, x, y, :, at]
+        s = full[k, x, y, :, at]
         for i in range(3):
             s = s + arcv[k, h, i].astype(F32)
         if k == 0:
@@ -296,7 +304,7 @@
             pltpu.VMEM((NK, 128, M), F32),
             pltpu.VMEM((NK, 128, M), F32),
             pltpu.VMEM((NK, 4, 4, ROWS, M), BF16),
-            pltpu.VMEM((2, 4, 4, ROWS, D), F32),
+            pltpu.VMEM((4, 4, 4, ROWS, D), F32),
             pltpu.VMEM((NK, 4, 4, ROWS, D), BF16),
             pltpu.VMEM((NK, 2, 2, 2, ROWS, HALF), BF16),
             pltpu.VMEM((NK, 2, 2, 4, ROWS, HALF), BF16),
@@ -306,8 +314,8 @@
             pltpu.VMEM((NK, ROWS, D), BF16),
             pltpu.VMEM((ROWS, D), F32),
             dma((3,)),
-            dma((NK, 2, 15)),
-            dma((NK, 2, 15)),
+            dma((NK, 2, 16)),
+            dma((NK, 2, 16)),
             dma((NK,)),
             dma((NK,)),
             dma((NK, 3)),
@@ -316,7 +324,7 @@
             dma((NK, 2, 10)),
         ],
         compiler_params=pltpu.CompilerParams(
-            collective_id=1, has_side_effects=True, vmem_limit_bytes=60 * 1024 * 1024
+            collective_id=1, has_side_effects=True, vmem_limit_bytes=61 * 1024 * 1024
         ),
         cost_estimate=pl.CostEstimate(flops=8 * 1024 * D * M, bytes_accessed=9 * 1024 * 1024, transcendentals=0),
         name="crosscoder",

time: 125 us -> 115 us (0.920); the launches traced: 122 us -> 115 us
  Pallas kernels: 121 us -> 113 us
    pallas_call x1, Pallas kernels: 121 us -> 113 us  [shards(): pl.pallas_call(kernel, out_shape=jax.ShapeDtypeStruct((ROWS, D), F32), in...]
where the time goes in v2:
time: 115 us
  Pallas kernels  113 us (98%)
  other arithmetic  1.68 us (1%)
    pallas_call x1, Pallas kernels, shards(): pl.pallas_call(kernel, out_shape=jax.ShapeDtypeStruct((ROWS, D), F32), in...  113 us

profile of v2, /device:TPU:1, one launch (start us, length us, event | category | flops | bytes accessed | tf_op | source)
XLA Modules:
  0.0 115.0 jit_solution(12555605298218855095)
XLA Ops:
  0.0 0.0 copy-start
  0.0 113.3 %crosscoder.1 = f32[16,4096]{1,0:T(8,128)} custom-call(bf16[1,16,4096]{2,1,0:T(8,128)(2,1)} %s_ref.1, bf16[1,4096,512]{2,1,0:T(8,128)(2,1)} %we_hbm.1, f32[1,512]{1,0:T(1,128)} %bitcast.5, bf16[1,512,4096]{2,1,0:T(8,128)(2,1)} %wd_hbm.1), custom_call_target="tpu_custom_call" | custom-call | flops 17179869184 | bytes 9437184 | tf_op jit(solution)/shard_map/crosscoder/pallas_call | solution.py:293
  113.4 0.0 copy-done
  113.4 1.7 %add_bitcast_fusion = f32[1,16,4096]{2,1,0:T(8,128)} fusion(f32[16,4096]{1,0:T(8,128)} %crosscoder.1, f32[4096]{0:T(1024)S(1)} %bitcast.4), kind=kLoop, calls=%fused_computation | loop fusion | flops 65536 | bytes 540672 | tf_op jit(solution)/shard_map/broadcast_in_dim | solution.py:332
Async XLA Ops:
  0.0 113.4 %copy-start = (f32[1,4096]{1,0:T(1,128)S(1)}, f32[1,4096]{1,0:T(1,128)}, u32[]{:S(2)}) copy-start(f32[1,4096]{1,0:T(1,128)} %param.9) | copy-start | bytes 49156

commit v3 on v2

v3 whole, which is shorter than its diff:
```python
import functools

import jax
import jax.numpy as jnp
from jax import lax
from jax.experimental import pallas as pl
from jax.experimental.pallas import tpu as pltpu
from jax.sharding import PartitionSpec as P

MESH = pl.DeviceIdType.MESH
F32, BF16 = jnp.float32, jnp.bfloat16
OFF = (0, 1, 3, 2)
NK = 4
ROWS, D, M, HALF = 16, 4096, 512, 2048
A_STEPS = (1, 3, 2)
EDGE = 256
SIDE = (D - EDGE) // 2
WHOLE = ()

PROGRAM = (
    "Z1", "Z2", "A0", "C00", "B01", "A1", "A2", "B11", "B10", "B21", "B12", "C10",
    "Z3", "C13", "C11", "B20", "C12", "B22", "A3", "C22", "C21", "C23", "C20", "D1",
    "B31", "X1", "B30", "B00", "D2", "X2", "C01", "B32", "B02", "Y1", "C31", "C33",
    "C30", "C32", "U1", "E10", "E11", "Y2", "C02", "D3", "C03", "U2", "E20", "X3",
    "E21", "D0", "F100", "F101", "F111", "F110", "F200", "Y3", "F201", "X0", "F210", "F211",
    "U3", "E30", "E31", "G21", "G11", "G10", "F300", "G20", "Y0", "F301", "F311", "F310",
    "E00", "E01", "H21", "H20", "G31", "G30", "H11", "H10", "F000", "F001", "F010", "F011",
    "H31", "H30", "G00", "G01", "H00", "H01",
)


def kernel(
    s_ref, we_hbm, eb_ref, wd_hbm, out_ref,
    g, we, wd, part, cx, q, zx, codes, full, ob, r1, r2, asnd, arcv, zsnd, zrcv, usnd, urcv, acc,
    lsem, ag_s, ag_r, zg_s, zg_r, x_s, x_r, rs_s, rs_r, u_s, u_r,
):
    lay, lat = lax.axis_index("layer"), lax.axis_index("latent")
    zlo, core = lay // 2, lay % 2
    x, y, z = lat // 16, (lat // 4) % 4, lat % 4
    m4 = lambda v: lax.rem(v + 8, 4)

    def dev(dx=0, dy=0, dz=0, dl=0, dc=0):
        return (
            lax.rem(zlo + dl, 2) * 2 + lax.rem(core + dc, 2),
            (m4(x + dx) * 4 + m4(y + dy)) * 4 + m4(z + dz),
        )

    def a_dev(h, d):
        return dev(dy=d) if h == 0 else dev(dx=d)

    def b_dev(h, d):
        return dev(dx=d) if h == 0 else dev(dy=d)

    ca = (y, x)
    cb = (x, y)
    cols = tuple(pl.ds(h * HALF, HALF) for h in range(2))

    def push(src, dst, ssem, rsem, target):
        return pltpu.make_async_remote_copy(
            src_ref=src, dst_ref=dst, send_sem=ssem, recv_sem=rsem, device_id=target, device_id_type=MESH
        )

    sent = []

    def start(copy):
        copy.start()
        sent.append(copy)

    load_s = [pltpu.make_async_copy(s_ref.at[0, :, cols[h]], g.at[0, h, cb[h], ca[h]], lsem.at[2 + h]) for h in range(2)]
    load_e = pltpu.make_async_copy(we_hbm.at[0], we, lsem.at[1])
    load_d = pltpu.make_async_copy(wd_hbm.at[0], wd, lsem.at[0])
    for copy in load_s:
        copy.start()
    load_e.start()
    load_d.start()
    bar = pltpu.get_barrier_semaphore()
    partners = [dev(dx=d) for d in (1, 2, 3)] + [dev(dy=d) for d in (1, 2, 3)]
    partners += [dev(dz=d) for d in (1, 2, 3)] + [dev(dc=1), dev(dl=1)]
    for p in partners:
        pl.semaphore_signal(bar, inc=1, device_id=p, device_id_type=MESH)
    pl.semaphore_wait(bar, len(partners))
    for copy in load_s:
        copy.wait()

    def zg(k, h):
        at = (h, cb[h], ca[h])
        return push(g.at[(0, *at)], g.at[(k, *at)], zg_s.at[k, h], zg_r.at[k, h], dev(dz=4 - OFF[k]))

    def ag(k, h, i):
        a, b = ca[h], cb[h]
        if i < 2:
            src, target = g.at[k, h, b, a], a_dev(h, A_STEPS[i])
        elif i == 2:
            src, target = g.at[k, h, b, m4(a + 3), :, pl.ds(0, HALF // 2)], a_dev(h, 1)
        elif i == 15:
            src, target = g.at[k, h, b, m4(a + 1), :, pl.ds(HALF // 2, HALF // 2)], a_dev(h, 3)
        elif k in WHOLE:
            way = 1 if i in (3, 11) else 3
            if i < 5:
                src = g.at[k, h, b]
            else:
                src = g.at[k, h, m4(b + 4 - way), pl.ds(0 if i == 11 else 2, 2)]
            target = b_dev(h, way)
        elif i < 11:
            j, way = (i - 3) // 2, (i - 3) % 2
            src, target = g.at[k, h, b, m4(a + j)], b_dev(h, 1 if way == 0 else 3)
        else:
            j = i - 11
            src = g.at[k, h, m4(b + (3 if j % 2 == 0 else 1)), m4(a + j)]
            target = b_dev(h, 1 if j % 2 == 0 else 3)
        return push(src, src, ag_s.at[k, h, i], ag_r.at[k, h, i], target)

    def step_z(k):
        for h in range(2):
            start(zg(k, h))

    def step_a(k):
        for h in range(2):
            if k:
                zg(k, h).wait_recv()
            for i in (0, 1) if k in WHOLE else (0, 1, 3, 4):
                start(ag(k, h, i))

    def step_b(k, i):
        j = (4 - A_STEPS[i]) % 4
        for h in range(2):
            ag(k, h, i).wait_recv()
            if i == 2:
                ag(k, h, 15).wait_recv()
            else:
                start(ag(k, h, 2 if i == 0 else 15))
            if k not in WHOLE:
                start(ag(k, h, 3 + 2 * j))
                start(ag(k, h, 4 + 2 * j))
            elif i == 2:
                start(ag(k, h, 3))
                start(ag(k, h, 4))

    def step_c(k, j):
        for h in range(2):
            ag(k, h, 3 + j if k in WHOLE else 3 + 2 * j + j % 2).wait_recv()
            start(ag(k, h, 11 + j))

    def step_w(k):
        for h in range(2):
            for j in range(0 if k in WHOLE else 4):
                ag(k, h, 3 + 2 * j + 1 - j % 2).wait_recv()
        for h in range(2):
            for j in range(2 if k in WHOLE else 4):
                ag(k, h, 11 + j).wait_recv()

    def xch(k, i):
        if i == 0:
            return push(part.at[k, 1 - core], cx.at[k], x_s.at[k, 0], x_r.at[k, 0], dev(dc=1))
        if i == 1:
            return push(q.at[k], zx.at[k], x_s.at[k, 1], x_r.at[k, 1], dev(dl=1))
        mine = codes.at[k, pl.ds(2 * core, 2)]
        return push(mine, mine, x_s.at[k, 2], x_r.at[k, 2], dev(dc=1))

    loaded = []

    def step_d(k):
        step_w(k)
        if not loaded:
            load_e.wait()
            load_d.wait()
            loaded.append(k)
        def body(n, c):
            at = pl.ds(pl.multiple_of(n * 256, 256), 256)
            r = jnp.dot(g[k, 0].reshape(256, HALF), we[cols[0], at], preferred_element_type=F32)
            lhs = jnp.concatenate([g[k, 1, :, i].reshape(64, HALF) for i in range(4)], axis=0)
            r = r + jnp.dot(lhs, we[cols[1], at], preferred_element_type=F32)
            part[k, :, :, at] = r.reshape(2, 128, 256)
            return c

        lax.fori_loop(0, 2, body, 0)
        start(xch(k, 0))

    def step_x(k):
        xch(k, 0).wait_recv()
        q[k] = part[k, core] + cx[k]
        start(xch(k, 1))

    def step_y(k):
        xch(k, 1).wait_recv()
        pre = q[k] + zx[k] + eb_ref[...]
        codes[k, pl.ds(2 * core, 2)] = jnp.maximum(pre, 0.0).astype(BF16).reshape(2, 4, ROWS, M)
        start(xch(k, 2))

    def wide(k):
        return HALF if k == 0 else SIDE

    def rs(k, h, i):
        a, b = ca[h], cb[h]
        at = pl.ds(0, wide(k))
        if i < 6:
            way = 1 if i % 2 == 0 else 3
            rows = pl.ds(2 if i in (1, 2, 5) else 0, 2)
            src = ob.at[k, h, m4(b + (2 if i < 2 else way)), rows, :, at]
            dst = r1.at[k, h, i, :, :, at] if i < 2 else r2.at[k, h, i % 2, rows, :, at]
            t = b_dev(h, way)
        elif i < 9:
            d = A_STEPS[i - 6]
            src, dst, t = asnd.at[k, h, m4(a + d), :, at], arcv.at[k, h, i - 6, :, at], a_dev(h, d)
        else:
            at = pl.ds(h * SIDE, SIDE)
            src, dst, t = zsnd.at[k, :, at], zrcv.at[k, :, at], dev(dz=OFF[k])
        return push(src, dst, rs_s.at[k, h, i], rs_r.at[k, h, i], t)

    def edge(k):
        return push(usnd.at[k], urcv.at[k], u_s.at[k], u_r.at[k], dev(dz=OFF[k]))

    def step_u(k):
        xch(k, 2).wait_recv()
        r = jnp.dot(codes[k].reshape(256, M), wd[:, pl.ds(2 * SIDE, EDGE)], preferred_element_type=F32)
        usnd[k] = r.reshape(4, 4, ROWS, EDGE).astype(BF16)
        start(edge(k))

    def tiles(width, step, body):
        def run(n, c):
            body(pl.multiple_of(n * step, step))
            return c

        lax.fori_loop(0, width // step, run, 0)

    def step_e(k, h):
        if k == 0 and h == 0:
            xch(k, 2).wait_recv()
        tile = 512 if k == 0 else 640

        def body(c0):
            at = pl.ds(c0, tile)
            r = jnp.dot(codes[k].reshape(256, M), wd[:, pl.ds(h * wide(k) + c0, tile)], preferred_element_type=F32)
            r = r.reshape(4, 4, ROWS, tile)
            if h == 0:
                full[k, 0, :, :, :, at] = r
                ob[k, 0, :, :, :, at] = r.astype(BF16)
            else:
                for i in range(4):
                    full[k, 1, :, i, :, at] = r[i]
                    ob[k, 1, :, i, :, at] = r[i].astype(BF16)

        tiles(wide(k), tile, body)
        if k == 0 and h == 1:
            at = pl.ds(HALF - EDGE, EDGE)
            for j in range(1, NK):
                edge(j).wait_recv()
            for i in range(4):
                r = full[0, 1, :, i, :, at]
                for j in range(1, NK):
                    r = r + urcv[j, i].astype(F32)
                full[0, 1, :, i, :, at] = r
                ob[0, 1, :, i, :, at] = r.astype(BF16)
        for i in range(4):
            start(rs(k, h, i))

    def step_f(k, h, w):
        rs(k, h, w).wait_recv()
        to = m4(cb[h] + (1 if w == 0 else 3))
        rows = pl.ds(0 if w == 0 else 2, 2)

        tile = 512 if k == 0 else 640

        def body(c0):
            at = pl.ds(c0, tile)
            got = r1[k, h, w, :, :, at].astype(F32)
            ob[k, h, to, rows, :, at] = (full[k, h, to, rows, :, at] + got).astype(BF16)

        tiles(wide(k), tile, body)
        start(rs(k, h, 4 + w))

    def step_g(k, h):
        for i in (2, 3, 4, 5):
            rs(k, h, i).wait_recv()
        b = cb[h]

        tile = 512 if k == 0 else 640

        def body(c0):
            at = pl.ds(c0, tile)
            got = r2[k, h, 0, :, :, at].astype(F32) + r2[k, h, 1, :, :, at].astype(F32)
            s = full[k, h, b, :, :, at] + got
            full[k, h, b, :, :, at] = s
            asnd[k, h, :, :, at] = s.astype(BF16)

        tiles(wide(k), tile, body)
        for i in (6, 7, 8):
            start(rs(k, h, i))

    def step_h(k, h):
        for i in (6, 7, 8):
            rs(k, h, i).wait_recv()
        at = pl.ds(0, wide(k))
        s = full[k, h, cb[h], ca[h], :, at]
        for i in range(3):
            s = s + arcv[k, h, i, :, at].astype(F32)
        if k == 0:
            acc[:, cols[h]] = s
        else:
            zsnd[k, :, pl.ds(h * SIDE, SIDE)] = s.astype(BF16)
            start(rs(k, h, 9))

    steps = dict(
        Z=step_z, A=step_a, B=step_b, C=step_c, D=step_d, X=step_x, Y=step_y, E=step_e, F=step_f, G=step_g, H=step_h,
        U=step_u,
    )
    for name in PROGRAM:
        steps[name[0]](*(int(v) for v in name[1:]))

    for k in range(1, NK):
        for h in range(2):
            rs(k, h, 9).wait_recv()
    at = pl.ds(0, 2 * SIDE)
    total = acc[:, at]
    for k in range(1, NK):
        total = total + zrcv[k, :, at].astype(F32)
    out_ref[:, at] = total
    at = pl.ds(2 * SIDE, EDGE)
    out_ref[:, at] = acc[:, at]
    for copy in sent:
        copy.wait_send()


def shards(streams, enc_weight, enc_bias, dec_weight, dec_bias):
    dma = pltpu.SemaphoreType.DMA
    any_space, vmem = pl.BlockSpec(memory_space=pl.ANY), pl.BlockSpec(memory_space=pltpu.VMEM)
    rows = pl.pallas_call(
        kernel,
        out_shape=jax.ShapeDtypeStruct((ROWS, D), F32),
        in_specs=[any_space, any_space, vmem, any_space],
        out_specs=vmem,
        scratch_shapes=[
            pltpu.VMEM((NK, 2, 4, 4, ROWS, HALF), BF16),
            pltpu.VMEM((D, M), BF16),
            pltpu.VMEM((M, D), BF16),
            pltpu.VMEM((NK, 2, 128, M), F32),
            pltpu.VMEM((NK, 128, M), F32),
            pltpu.VMEM((NK, 128, M), F32),
            pltpu.VMEM((NK, 128, M), F32),
            pltpu.VMEM((NK, 4, 4, ROWS, M), BF16),
            pltpu.VMEM((NK, 2, 4, 4, ROWS, HALF), F32),
            pltpu.VMEM((NK, 2, 4, 4, ROWS, HALF), BF16),
            pltpu.VMEM((NK, 2, 2, 2, ROWS, HALF), BF16),
            pltpu.VMEM((NK, 2, 2, 4, ROWS, HALF), BF16),
            pltpu.VMEM((NK, 2, 4, ROWS, HALF), BF16),
            pltpu.VMEM((NK, 2, 3, ROWS, HALF), BF16),
            pltpu.VMEM((NK, ROWS, D), BF16),
            pltpu.VMEM((NK, ROWS, D), BF16),
            pltpu.VMEM((NK, 4, 4, ROWS, EDGE), BF16),
            pltpu.VMEM((NK, 4, 4, ROWS, EDGE), BF16),
            pltpu.VMEM((ROWS, D), F32),
            dma((4,)),
            dma((NK, 2, 16)),
            dma((NK, 2, 16)),
            dma((NK, 2)),
            dma((NK, 2)),
            dma((NK, 3)),
            dma((NK, 3)),
            dma((NK, 2, 10)),
            dma((NK, 2, 10)),
            dma((NK,)),
            dma((NK,)),
        ],
        compiler_params=pltpu.CompilerParams(
            collective_id=1, has_side_effects=True, vmem_limit_bytes=61 * 1024 * 1024
        ),
        cost_estimate=pl.CostEstimate(flops=8 * 1024 * D * M, bytes_accessed=9 * 1024 * 1024, transcendentals=0),
        name="crosscoder",
    )(streams, enc_weight, enc_bias.reshape(1, M), dec_weight)
    return (rows + dec_bias)[None]


def solution(mesh):
    in_specs = (
        P("layer", "latent", None),
        P("layer", None, "latent"),
        P("latent"),
        P("layer", "latent", None),
        P("layer", None),
    )
    return jax.shard_map(
        shards, mesh=mesh, in_specs=in_specs, out_specs=P("layer", "latent", None), check_vma=False
    )
```

time: 115 us -> 116 us (level)
  no operation moved by 1% of the time
where the time goes in v3:
time: 116 us
  Pallas kernels  114 us (98%)
  other arithmetic  1.68 us (1%)
    pallas_call x1, Pallas kernels, shards(): pl.pallas_call(kernel, out_shape=jax.ShapeDtypeStruct((ROWS, D), F32), in...  114 us

profile of v3, /device:TPU:1, one launch (start us, length us, event | category | flops | bytes accessed | tf_op | source)
XLA Modules:
  0.0 115.8 jit_solution(8468654676044682083)
XLA Ops:
  0.0 0.0 copy-start
  0.0 114.1 %crosscoder.1 = f32[16,4096]{1,0:T(8,128)} custom-call(bf16[1,16,4096]{2,1,0:T(8,128)(2,1)} %s_ref.1, bf16[1,4096,512]{2,1,0:T(8,128)(2,1)} %we_hbm.1, f32[1,512]{1,0:T(1,128)} %bitcast.5, bf16[1,512,4096]{2,1,0:T(8,128)(2,1)} %wd_hbm.1), custom_call_target="tpu_custom_call" | custom-call | flops 17179869184 | bytes 9437184 | tf_op jit(solution)/shard_map/crosscoder/pallas_call | solution.py:327
  114.2 0.0 copy-done
  114.2 1.7 %add_bitcast_fusion = f32[1,16,4096]{2,1,0:T(8,128)} fusion(f32[16,4096]{1,0:T(8,128)} %crosscoder.1, f32[4096]{0:T(1024)S(1)} %bitcast.4), kind=kLoop, calls=%fused_computation | loop fusion | flops 65536 | bytes 540672 | tf_op jit(solution)/shard_map/broadcast_in_dim | solution.py:370
Async XLA Ops:
  0.0 114.2 %copy-start = (f32[1,4096]{1,0:T(1,128)S(1)}, f32[1,4096]{1,0:T(1,128)}, u32[]{:S(2)}) copy-start(f32[1,4096]{1,0:T(1,128)} %param.9) | copy-start | bytes 49156

commit v4 on v2

--- a/solution.py
+++ b/solution.py
@@ -15,14 +15,14 @@
 A_STEPS = (1, 3, 2)
 
 PROGRAM = (
-    "Z2", "A0", "Z1", "B00", "B01", "A1", "B02", "A2", "C00", "B10", "Z3", "B11",
-    "C03", "C01", "C02", "B12", "A3", "B20", "C11", "C13", "C12", "C10", "D0", "X0",
-    "B31", "B30", "B21", "B32", "D1", "C33", "C31", "B22", "Y0", "X1", "C30", "C32",
-    "C21", "C22", "C20", "C23", "E00", "E01", "D3", "Y1", "X3", "E10", "E11", "D2",
-    "X2", "F010", "F000", "F011", "Y3", "F001", "E30", "E31", "Y2", "E20", "E21", "F101",
-    "F100", "F300", "F310", "F301", "F311", "F111", "F110", "F201", "F200", "F211", "F210", "G31",
-    "G30", "G20", "G11", "H31", "G10", "H30", "G21", "H20", "H11", "H21", "H10", "G01",
-    "G00", "H01", "H00",
+    "A0", "Z3", "B00", "B01", "Z2", "C00", "Z1", "A3", "C03", "B02", "A2", "B31",
+    "C01", "A1", "B30", "C02", "C31", "B20", "B32", "B11", "C33", "C30", "D0", "C32",
+    "X0", "B10", "C11", "B21", "C13", "B12", "D3", "C10", "B22", "C23", "Y0", "X3",
+    "C12", "E00", "C20", "E01", "D1", "X1", "C21", "Y3", "C22", "E30", "E31", "F000",
+    "F001", "D2", "F011", "F010", "X2", "Y1", "E10", "E11", "F300", "F311", "F310", "F301",
+    "Y2", "E20", "E21", "F111", "F110", "G31", "G30", "F201", "F200", "F210", "F211", "F101",
+    "F100", "H31", "G11", "G20", "H30", "G21", "G10", "H11", "H20", "G00", "G01", "H21",
+    "H10", "H01", "H00",
 )
 
 

time: 115 us -> 113 us (0.983)
  Pallas kernels: 113 us -> 111 us
    pallas_call x1, Pallas kernels: 113 us -> 111 us  [shards(): pl.pallas_call(kernel, out_shape=jax.ShapeDtypeStruct((ROWS, D), F32), in...]
where the time goes in v4:
time: 113 us
  Pallas kernels  111 us (98%)
  other arithmetic  1.68 us (1%)
    pallas_call x1, Pallas kernels, shards(): pl.pallas_call(kernel, out_shape=jax.ShapeDtypeStruct((ROWS, D), F32), in...  111 us

profile of v4, /device:TPU:1, one launch (start us, length us, event | category | flops | bytes accessed | tf_op | source)
XLA Modules:
  0.0 112.8 jit_solution(18164016585455164453)
XLA Ops:
  0.0 0.0 copy-start
  0.0 111.1 %crosscoder.1 = f32[16,4096]{1,0:T(8,128)} custom-call(bf16[1,16,4096]{2,1,0:T(8,128)(2,1)} %s_ref.1, bf16[1,4096,512]{2,1,0:T(8,128)(2,1)} %we_hbm.1, f32[1,512]{1,0:T(1,128)} %bitcast.5, bf16[1,512,4096]{2,1,0:T(8,128)(2,1)} %wd_hbm.1), custom_call_target="tpu_custom_call" | custom-call | flops 17179869184 | bytes 9437184 | tf_op jit(solution)/shard_map/crosscoder/pallas_call | solution.py:293
  111.1 0.0 copy-done
  111.1 1.7 %add_bitcast_fusion = f32[1,16,4096]{2,1,0:T(8,128)} fusion(f32[16,4096]{1,0:T(8,128)} %crosscoder.1, f32[4096]{0:T(1024)S(1)} %bitcast.4), kind=kLoop, calls=%fused_computation | loop fusion | flops 65536 | bytes 540672 | tf_op jit(solution)/shard_map/broadcast_in_dim | solution.py:332
Async XLA Ops:
  0.0 111.1 %copy-start = (f32[1,4096]{1,0:T(1,128)S(1)}, f32[1,4096]{1,0:T(1,128)}, u32[]{:S(2)}) copy-start(f32[1,4096]{1,0:T(1,128)} %param.9) | copy-start | bytes 49156

commit v5 on v4

--- a/solution.py
+++ b/solution.py
@@ -90,6 +90,8 @@
         a, b = ca[h], cb[h]
         if i < 2:
             src, target = slot(g, k, h, b, a), a_dev(h, A_STEPS[i])
+        elif k == 0 and i == 2:
+            src, target = slot(g, k, h, b, a), a_dev(h, 2)
         elif i == 2 or i == 15:
             from_a, w = (m4(a + 3), 0) if i == 2 else (m4(a + 1), 1)
             at = pl.ds(h * HALF + w * (HALF // 2), HALF // 2)
@@ -111,16 +113,16 @@
         if k:
             zg(k).wait_recv()
         for h in range(2):
-            for i in (0, 1, 3, 4):
+            for i in (0, 1, 3, 4, 2) if k == 0 else (0, 1, 3, 4):
                 start(ag(k, h, i))
 
     def step_b(k, i):
         j = (4 - A_STEPS[i]) % 4
         for h in range(2):
             ag(k, h, i).wait_recv()
-            if i == 2:
+            if k and i == 2:
                 ag(k, h, 15).wait_recv()
-            else:
+            elif k:
                 start(ag(k, h, 2 if i == 0 else 15))
             start(ag(k, h, 3 + 2 * j))
             start(ag(k, h, 4 + 2 * j))

time: 113 us -> 113 us (level)
  no operation moved by 1% of the time
where the time goes in v5:
time: 113 us
  Pallas kernels  111 us (98%)
  other arithmetic  1.68 us (1%)
    pallas_call x1, Pallas kernels, shards(): pl.pallas_call(kernel, out_shape=jax.ShapeDtypeStruct((ROWS, D), F32), in...  111 us

profile of v5, /device:TPU:1, one launch (start us, length us, event | category | flops | bytes accessed | tf_op | source)
XLA Modules:
  0.0 112.8 jit_solution(2577721229659617849)
XLA Ops:
  0.0 0.0 copy-start
  0.0 111.1 %crosscoder.1 = f32[16,4096]{1,0:T(8,128)} custom-call(bf16[1,16,4096]{2,1,0:T(8,128)(2,1)} %s_ref.1, bf16[1,4096,512]{2,1,0:T(8,128)(2,1)} %we_hbm.1, f32[1,512]{1,0:T(1,128)} %bitcast.5, bf16[1,512,4096]{2,1,0:T(8,128)(2,1)} %wd_hbm.1), custom_call_target="tpu_custom_call" | custom-call | flops 17179869184 | bytes 9437184 | tf_op jit(solution)/shard_map/crosscoder/pallas_call | solution.py:295
  111.1 0.0 copy-done
  111.1 1.7 %add_bitcast_fusion = f32[1,16,4096]{2,1,0:T(8,128)} fusion(f32[16,4096]{1,0:T(8,128)} %crosscoder.1, f32[4096]{0:T(1024)S(1)} %bitcast.4), kind=kLoop, calls=%fused_computation | loop fusion | flops 65536 | bytes 540672 | tf_op jit(solution)/shard_map/broadcast_in_dim | solution.py:334
Async XLA Ops:
  0.0 111.1 %copy-start = (f32[1,4096]{1,0:T(1,128)S(1)}, f32[1,4096]{1,0:T(1,128)}, u32[]{:S(2)}) copy-start(f32[1,4096]{1,0:T(1,128)} %param.9) | copy-start | bytes 49156

commit v6 on v5

--- a/solution.py
+++ b/solution.py
@@ -229,14 +229,14 @@
         rows = pl.ds(0 if w == 0 else 2, 2)
 
         def body(c0):
-            at = pl.ds(h * HALF + c0, 512)
-            got = r1[k, h, w, :, :, pl.ds(c0, 512)].astype(F32)
+            at = pl.ds(h * HALF + c0, 1024)
+            got = r1[k, h, w, :, :, pl.ds(c0, 1024)].astype(F32)
             if h == 0:
                 ob[k, to, rows, :, at] = (full[k, to, rows, :, at] + got).astype(BF16)
             else:
                 ob[k, rows, to, :, at] = (full[k, rows, to, :, at] + got).astype(BF16)
 
-        tiles(HALF, 512, body)
+        tiles(HALF, 1024, body)
         start(rs(k, h, 4 + w))
 
     def step_g(k, h):
@@ -245,17 +245,17 @@
         b = cb[h]
 
         def body(c0):
-            at = pl.ds(h * HALF + c0, 512)
-            got = r2[k, h, 0, :, :, pl.ds(c0, 512)].astype(F32) + r2[k, h, 1, :, :, pl.ds(c0, 512)].astype(F32)
+            at = pl.ds(h * HALF + c0, 1024)
+            got = r2[k, h, 0, :, :, pl.ds(c0, 1024)].astype(F32) + r2[k, h, 1, :, :, pl.ds(c0, 1024)].astype(F32)
             if h == 0:
                 s = full[k, b, :, :, at] + got
                 full[k, b, :, :, at] = s
             else:
                 s = full[k, :, b, :, at] + got
                 full[k, :, b, :, at] = s
-            asnd[k, h, :, :, pl.ds(c0, 512)] = s.astype(BF16)
-
-        tiles(HALF, 512, body)
+            asnd[k, h, :, :, pl.ds(c0, 1024)] = s.astype(BF16)
+
+        tiles(HALF, 1024, body)
         for i in (6, 7, 8):
             start(rs(k, h, i))
 

time: 113 us -> 113 us (level)
  no operation moved by 1% of the time
where the time goes in v6:
time: 113 us
  Pallas kernels  111 us (98%)
  other arithmetic  1.68 us (1%)
    pallas_call x1, Pallas kernels, shards(): pl.pallas_call(kernel, out_shape=jax.ShapeDtypeStruct((ROWS, D), F32), in...  111 us

profile of v6, /device:TPU:1, one launch (start us, length us, event | category | flops | bytes accessed | tf_op | source)
XLA Modules:
  0.0 112.8 jit_solution(8750157949354301533)
XLA Ops:
  0.0 0.0 copy-start
  0.0 111.1 %crosscoder.1 = f32[16,4096]{1,0:T(8,128)} custom-call(bf16[1,16,4096]{2,1,0:T(8,128)(2,1)} %s_ref.1, bf16[1,4096,512]{2,1,0:T(8,128)(2,1)} %we_hbm.1, f32[1,512]{1,0:T(1,128)} %bitcast.5, bf16[1,512,4096]{2,1,0:T(8,128)(2,1)} %wd_hbm.1), custom_call_target="tpu_custom_call" | custom-call | flops 17179869184 | bytes 9437184 | tf_op jit(solution)/shard_map/crosscoder/pallas_call | solution.py:295
  111.1 0.0 copy-done
  111.1 1.7 %add_bitcast_fusion = f32[1,16,4096]{2,1,0:T(8,128)} fusion(f32[16,4096]{1,0:T(8,128)} %crosscoder.1, f32[4096]{0:T(1024)S(1)} %bitcast.4), kind=kLoop, calls=%fused_computation | loop fusion | flops 65536 | bytes 540672 | tf_op jit(solution)/shard_map/broadcast_in_dim | solution.py:334
Async XLA Ops:
  0.0 111.1 %copy-start = (f32[1,4096]{1,0:T(1,128)S(1)}, f32[1,4096]{1,0:T(1,128)}, u32[]{:S(2)}) copy-start(f32[1,4096]{1,0:T(1,128)} %param.9) | copy-start | bytes 49156

commit v7 on v5

--- a/solution.py
+++ b/solution.py
@@ -205,14 +205,14 @@
             xch(k, 2).wait_recv()
 
         def body(n, c):
-            at = pl.ds(pl.multiple_of(h * HALF + n * 512, 512), 512)
+            at = pl.ds(pl.multiple_of(h * HALF + n * 1024, 1024), 1024)
             r = jnp.dot(codes[k].reshape(256, M), wd[:, at], preferred_element_type=F32)
-            r = r.reshape(4, 4, ROWS, 512)
+            r = r.reshape(4, 4, ROWS, 1024)
             full[k, :, :, :, at] = r
             ob[k, :, :, :, at] = r.astype(BF16)
             return c
 
-        lax.fori_loop(0, HALF // 512, body, 0)
+        lax.fori_loop(0, HALF // 1024, body, 0)
         for i in range(4):
             start(rs(k, h, i))
 

time: 113 us -> 113 us (level)
  no operation moved by 1% of the time
where the time goes in v7:
time: 113 us
  Pallas kernels  111 us (98%)
  other arithmetic  1.68 us (1%)
    pallas_call x1, Pallas kernels, shards(): pl.pallas_call(kernel, out_shape=jax.ShapeDtypeStruct((ROWS, D), F32), in...  111 us

profile of v7, /device:TPU:1, one launch (start us, length us, event | category | flops | bytes accessed | tf_op | source)
XLA Modules:
  0.0 112.6 jit_solution(18278295926284082373)
XLA Ops:
  0.0 0.0 copy-start
  0.0 110.9 %crosscoder.1 = f32[16,4096]{1,0:T(8,128)} custom-call(bf16[1,16,4096]{2,1,0:T(8,128)(2,1)} %s_ref.1, bf16[1,4096,512]{2,1,0:T(8,128)(2,1)} %we_hbm.1, f32[1,512]{1,0:T(1,128)} %bitcast.5, bf16[1,512,4096]{2,1,0:T(8,128)(2,1)} %wd_hbm.1), custom_call_target="tpu_custom_call" | custom-call | flops 17179869184 | bytes 9437184 | tf_op jit(solution)/shard_map/crosscoder/pallas_call | solution.py:295
  110.9 0.0 copy-done
  111.0 1.7 %add_bitcast_fusion = f32[1,16,4096]{2,1,0:T(8,128)} fusion(f32[16,4096]{1,0:T(8,128)} %crosscoder.1, f32[4096]{0:T(1024)S(1)} %bitcast.4), kind=kLoop, calls=%fused_computation | loop fusion | flops 65536 | bytes 540672 | tf_op jit(solution)/shard_map/broadcast_in_dim | solution.py:334
Async XLA Ops:
  0.0 110.9 %copy-start = (f32[1,4096]{1,0:T(1,128)S(1)}, f32[1,4096]{1,0:T(1,128)}, u32[]{:S(2)}) copy-start(f32[1,4096]{1,0:T(1,128)} %param.9) | copy-start | bytes 49156
